TPU v7x, 128 devices: a whole 4x4x4 slice. The times are simulated.
128 devices in a mesh: ha: 16 (over x, y_hi, core), wa: 8 (over y_lo, z).
Axes of the slice: x: 4, y: 4 (y_hi: 2, y_lo: 2; y = y_hi * 2 + y_lo), z: 4, core: 2. Of those that a mesh axis runs over, the one named last changes fastest.
Arguments:
- latent_map: bfloat16 [384, 128, 160], P('wa', 'ha'), may hold values from -6 to 6
- coarse_cache: bfloat16 [2, 384, 128, 160], P(None, 'wa', 'ha'), may hold values from -6 to 6
- coarse_gain: float32 [384], replicated, may hold values from 0.1 to 1.9
- coarse_kernel: bfloat16 [3, 3, 3, 384, 384], replicated, may hold values from -0.0625 to 0.0625
- coarse_bias: float32 [384], replicated, may hold values from -3 to 3
- upper_kernel: bfloat16 [3, 3, 192, 384], replicated, may hold values from -0.109375 to 0.109375
- upper_bias: float32 [192], replicated, may hold values from -3 to 3
- middle_cache: bfloat16 [2, 192, 256, 320], P(None, None, 'ha', 'wa'), may hold values from -6 to 6
- middle_gain: float32 [192], replicated, may hold values from 0.1 to 1.9
- middle_kernel: bfloat16 [3, 3, 3, 384, 192], replicated, may hold values from -0.078125 to 0.078125
- middle_bias: float32 [384], replicated, may hold values from -3 to 3
- bypass_weight: bfloat16 [384, 192], replicated, may hold values from -0.4375 to 0.4375
- bypass_bias: float32 [384], replicated, may hold values from -3 to 3
- finer_kernel: bfloat16 [3, 3, 192, 384], replicated, may hold values from -0.109375 to 0.109375
- finer_bias: float32 [192], replicated, may hold values from -3 to 3
- fine_cache: bfloat16 [2, 192, 512, 640], P(None, None, 'ha', 'wa'), may hold values from -6 to 6
- fine_gain: float32 [192], replicated, may hold values from 0.1 to 1.9
- fine_kernel: bfloat16 [3, 3, 3, 192, 192], replicated, may hold values from -0.078125 to 0.078125
- fine_bias: float32 [192], replicated, may hold values from -3 to 3
Outputs:
- fine_map: bfloat16 [192, 512, 640], P(None, 'ha', 'wa')
All inputs are finite; a program needn't handle non-finite values.
Results may differ from a plain program's by a relative error of at most 0.0095.
Values may be sent and summed in bfloat16 or wider, within the bound.
A program may use at most 320 MiB of HBM per device.

v0:
```python
import jax
import jax.numpy as jnp
from jax import lax
from jax.sharding import PartitionSpec as P


def padded(x, sides, width):
    for axis, dim in sides:
        size, length = (lax.axis_size(axis), x.shape[dim])
        up = [(i, (i + 1) % size) for i in range(size - 1)]
        down = [(j, i) for i, j in up]
        last = lax.slice_in_dim(x, length - width, length, axis=dim)
        leading = lax.slice_in_dim(x, 0, width, axis=dim)
        before = lax.ppermute(last, axis, up)
        after = lax.ppermute(leading, axis, down)
        x = jnp.concatenate([before, x, after], axis=dim)
    return x


def activate(values, gain):
    wide = values.astype(jnp.float32)
    meansq = jnp.mean(wide * wide, axis=0, keepdims=True)
    return jax.nn.silu(wide * lax.rsqrt(meansq + 1e-06) * gain[:, None, None]).astype(jnp.bfloat16)


def enlarge(values):
    return jnp.repeat(jnp.repeat(values, 2, axis=1), 2, axis=2)


def convolve(frames, kernel, height, width):
    total = jnp.zeros((kernel.shape[3], height, width), jnp.float32)
    for frame_index in range(kernel.shape[0]):
        for row_tap in range(3):
            for col_tap in range(3):
                piece = frames[
                    frame_index, :, row_tap : row_tap + height, col_tap : col_tap + width
                ]
                total = total + jnp.einsum(
                    "oi,irw->orw",
                    kernel[frame_index, row_tap, col_tap],
                    piece,
                    preferred_element_type=jnp.float32,
                )
    return total


def keep_inside(values, first_row, total_rows, first_col, total_cols):
    row_ids = first_row + jnp.arange(values.shape[1])
    col_ids = first_col + jnp.arange(values.shape[2])
    inside = ((row_ids >= 0) & (row_ids < total_rows))[:, None] & (
        (col_ids >= 0) & (col_ids < total_cols)
    )[None, :]
    return jnp.where(inside[None], values, 0.0)


def per_device(
    latent_map,
    coarse_cache,
    coarse_gain,
    coarse_kernel,
    coarse_bias,
    upper_kernel,
    upper_bias,
    middle_cache,
    middle_gain,
    middle_kernel,
    middle_bias,
    bypass_weight,
    bypass_bias,
    finer_kernel,
    finer_bias,
    fine_cache,
    fine_gain,
    fine_kernel,
    fine_bias,
):
    slab_rows = latent_map.shape[1]
    latent_width = latent_map.shape[2]
    strip_cols = latent_width // lax.axis_size("wa")
    latent_height = slab_rows * lax.axis_size("ha")
    row_base = lax.axis_index("ha") * slab_rows
    col_base = lax.axis_index("wa") * strip_cols
    margin_cells = 1
    reach_cells = margin_cells + 1
    out_rows = slab_rows + 2 * margin_cells
    out_cols = strip_cols + 2 * margin_cells
    stacked = jnp.concatenate([coarse_cache, latent_map[None]], 0)
    gathered = lax.all_gather(stacked, "wa", axis=1, tiled=True)
    framed = padded(gathered, (("ha", 2),), reach_cells)
    framed = jnp.pad(framed, ((0, 0), (0, 0), (0, 0), (1, 1)))
    residual_in = framed[2, :, 1 : out_rows + 1, 1 : latent_width + 1]
    inputs = jnp.concatenate([framed[:2], activate(framed[2], coarse_gain)[None]], 0)
    summed = (
        residual_in.astype(jnp.float32)
        + convolve(inputs, coarse_kernel, out_rows, latent_width)
        + coarse_bias[:, None, None]
    )
    summed = jnp.pad(summed, ((0, 0), (0, 0), (margin_cells, margin_cells)))
    summed = lax.dynamic_slice_in_dim(summed, col_base, out_cols, 2)
    window = keep_inside(
        summed, row_base - margin_cells, latent_height, col_base - margin_cells, latent_width
    ).astype(jnp.bfloat16)
    mid_rows = 2 * slab_rows
    mid_cols = 2 * strip_cols
    fine_rows = 2 * mid_rows
    fine_cols = 2 * mid_cols
    enlarged = enlarge(window)[:, 1 : mid_rows + 3, 1 : mid_cols + 3]
    up_mid = (
        convolve(enlarged[None], upper_kernel[None], mid_rows, mid_cols) + upper_bias[:, None, None]
    ).astype(jnp.bfloat16)
    frames_mid = jnp.concatenate([middle_cache, activate(up_mid, middle_gain)[None]], 0)
    framed_mid = padded(frames_mid, (("ha", 2), ("wa", 3)), 1)
    bypass = jnp.einsum("oi,irw->orw", bypass_weight, up_mid, preferred_element_type=jnp.float32)
    middle = (
        bypass
        + bypass_bias[:, None, None]
        + convolve(framed_mid, middle_kernel, mid_rows, mid_cols)
        + middle_bias[:, None, None]
    ).astype(jnp.bfloat16)
    bordered = padded(middle, (("ha", 1), ("wa", 2)), 1)
    enlarged_fine = enlarge(bordered)[:, 1 : fine_rows + 3, 1 : fine_cols + 3]
    up_fine = (
        convolve(enlarged_fine[None], finer_kernel[None], fine_rows, fine_cols)
        + finer_bias[:, None, None]
    ).astype(jnp.bfloat16)
    frames_fine = jnp.concatenate([fine_cache, activate(up_fine, fine_gain)[None]], 0)
    framed_fine = padded(frames_fine, (("ha", 2), ("wa", 3)), 1)
    fine_map = (
        up_fine.astype(jnp.float32)
        + convolve(framed_fine, fine_kernel, fine_rows, fine_cols)
        + fine_bias[:, None, None]
    ).astype(jnp.bfloat16)
    return fine_map


def solution(mesh):
    placed = (
        P("wa", "ha", None),
        P(None, "wa", "ha", None),
        P(),
        P(),
        P(),
        P(),
        P(),
        P(None, None, "ha", "wa"),
        P(),
        P(),
        P(),
        P(),
        P(),
        P(),
        P(),
        P(None, None, "ha", "wa"),
        P(),
        P(),
        P(),
    )
    return jax.shard_map(
        per_device, mesh=mesh, in_specs=placed, out_specs=P(None, "ha", "wa"), check_vma=False
    )
```

profile of v0, /device:TPU:99, one launch (start us, length us, event | category | flops | bytes accessed | tf_op | source)
XLA Modules:
  0.0 376.7 jit_solution(6237900655016839007)
XLA Ops:
  6.5 2.0 pad_maximum_fusion.12
  9.8 2.2 fusion.284
  12.0 53.3 %all-gather.2.cloned.1.call-done = bf16[3,384,8,160]{3,2,0,1:T(8,128)(2,1)} async-done(((bf16[3,48,8,160]{3,2,0,1:T(8,128)(2,1)}), bf16[3,384,8,160]{3,2,0,1:T(8,128)(2,1)}) %all-gather.2.cloned.1.call-update) | async-done | bytes 2949136 | tf_op jit(solution)/shard_map/all_gather | solution.py:88
  65.3 6.7 %copy.23 = bf16[3,384,8,160]{1,3,2,0:T(8,128)(2,1)} copy(bf16[3,384,8,160]{3,2,0,1:T(8,128)(2,1)} %all-gather.2.cloned.1.call-done) | data formatting | bytes 5898240 | tf_op jit(solution)/shard_map/all_gather | solution.py:88
  73.6 5.0 %collective-permute-start = (bf16[3,384,2,160]{1,3,2,0:T(8,128)(2,1)S(1)}, bf16[3,384,2,160]{1,3,2,0:T(8,128)(2,1)S(1)}, u32[]{:S(2)}, u32[]{:S(2)}) collective-permute-start(bf16[3,384,2,160]{1,3,2,0:T(8,128)(2,1)S(1)} %get-tuple-element.11), channel_id=1, source_target_pairs={{0,8},{8,16},{16,24},{24,32},{32,40},{40,48},{48,56},{56,64},{64,7... | collective-permute-start | bytes 2211848 | tf_op jit(solution)/shard_map/ppermute | solution.py:14
  80.6 2.2 fusion.282
  84.4 10.4 %collective-permute-done = bf16[3,384,2,160]{1,3,2,0:T(8,128)(2,1)S(1)} collective-permute-done((bf16[3,384,2,160]{1,3,2,0:T(8,128)(2,1)S(1)}, bf16[3,384,2,160]{1,3,2,0:T(8,128)(2,1)S(1)}, u32[]{:S(2)}, u32[]{:S(2)}) %collective-permute-start) | collective-permute-done | bytes 737312 | tf_op jit(solution)/shard_map/ppermute | solution.py:14
  100.2 2.4 fusion.105
  102.6 2.4 fusion.106
  105.0 2.4 fusion.107
  107.4 2.4 fusion.108
  109.8 2.4 fusion.109
  112.2 2.3 fusion.110
  114.6 2.3 fusion.111
  116.9 2.3 fusion.112
  119.3 2.3 fusion.117
  121.6 2.4 fusion.125
  124.0 2.4 fusion.129
  126.4 2.5 fusion.131
  128.9 2.5 fusion.133
  131.4 2.4 fusion.135
  133.7 2.7 fusion.137
  136.4 2.4 fusion.139
  138.8 2.4 fusion.141
  141.2 2.3 fusion.143
  143.6 2.4 fusion.145
  146.0 2.4 fusion.147
  148.3 2.4 fusion.149
  150.7 2.4 fusion.151
  153.1 2.4 fusion.114
  155.5 2.3 fusion.119
  157.8 2.4 fusion.122
  160.3 2.4 fusion.126
  162.7 23.9 %fusion.20 = bf16[384,10,160]{0,2,1:T(8,128)(2,1)} fusion(f32[10,160,384]{2,1,0:T(8,128)} %fusion.105, f32[10,160,384]{2,1,0:T(8,128)} %fusion.106, f32[10,160,384]{2,1,0:T(8,128)} %fusion.107, f32[10,160,384]{2,1,0:T(8,128)} %fusion.108, f32[10,160,384]{2,1,0:T(8,128)} %fusion.109, f32[10,160,384]{2,1,0:T(8,128)} %fusion.110, ...), kind=kOutput, calls=%fused_computation.52 | convolution fusion | flops 490291200 | bytes 67880448 | tf_op jit(solution)/shard_map/oi,irw->orw/dot_general | solution.py:38
  195.3 4.3 %collective-permute-start.2 = (bf16[3,192,1,40]{1,3,2,0:T(8,128)(2,1)S(1)}, bf16[3,192,1,40]{1,3,2,0:T(8,128)(2,1)S(1)}, u32[]{:S(2)}, u32[]{:S(2)}) collective-permute-start(bf16[3,192,1,40]{1,3,2,0:T(8,128)(2,1)S(1)} %get-tuple-element.19), channel_id=1, source_target_pairs={{0,8},{8,16},{16,24},{24,32},{32,40},{40,48},{48,56},{56,64},{64,7... | collective-permute-start | bytes 138248 | tf_op jit(solution)/shard_map/ppermute | solution.py:14
  201.9 4.7 %collective-permute-done.3 = bf16[3,192,1,40]{1,3,2,0:T(8,128)(2,1)S(1)} collective-permute-done((bf16[3,192,1,40]{1,3,2,0:T(8,128)(2,1)S(1)}, bf16[3,192,1,40]{1,3,2,0:T(8,128)(2,1)S(1)}, u32[]{:S(2)}, u32[]{:S(2)}) %collective-permute-start.3) | collective-permute-done | bytes 46112 | tf_op jit(solution)/shard_map/ppermute | solution.py:15
  206.7 4.3 %collective-permute-start.4 = (bf16[3,192,18,1]{1,3,2,0:T(2,128)(2,1)S(1)}, bf16[3,192,18,1]{1,3,2,0:T(2,128)(2,1)S(1)}, u32[]{:S(2)}, u32[]{:S(2)}) collective-permute-start(bf16[3,192,18,1]{1,3,2,0:T(2,128)(2,1)S(1)} %get-tuple-element.17), channel_id=1, source_target_pairs={{0,1},{1,2},{2,3},{3,4},{4,5},{5,6},{6,7},{8,9},{9,10},{10,11},{11... | collective-permute-start | bytes 62216 | tf_op jit(solution)/shard_map/ppermute | solution.py:14
  215.0 3.0 collective-permute-done.5
  227.3 4.0 %collective-permute-start.6 = (bf16[384,1,40]{0,2,1:T(8,128)(2,1)S(1)}, bf16[384,1,40]{0,2,1:T(8,128)(2,1)S(1)}, u32[]{:S(2)}, u32[]{:S(2)}) collective-permute-start(bf16[384,1,40]{0,2,1:T(8,128)(2,1)S(1)} %get-tuple-element.25), channel_id=1, source_target_pairs={{0,8},{8,16},{16,24},{24,32},{32,40},{40,48},{48,56},{56,64},{64,7... | collective-permute-start | bytes 92168 | tf_op jit(solution)/shard_map/ppermute | solution.py:14
  233.3 2.9 fusion.342
  240.0 3.4 collective-permute-start.9
  243.4 3.0 fusion.340
  247.2 2.6 broadcast_in_dim.70
  249.8 6.3 %reshape.93 = bf16[384,36,84]{0,2,1:T(8,128)(2,1)} reshape(bf16[384,36,42,2]{0,3,2,1:T(2,128)(2,1)} %broadcast_in_dim.70) | data formatting | bytes 4644864 | tf_op jit(solution)/shard_map/reshape | solution.py:27
  256.1 2.9 slice_bitcast_fusion
  261.6 2.4 fusion.24
  265.7 2.4 fusion.27
  269.1 4.6 %fusion.12 = (f32[32,80]{1,0:T(8,128)S(1)}, bf16[32,80,192]{2,1,0:T(8,128)(2,1)S(1)}) fusion(f32[192]{0:T(256)S(1)} %copy-done.21, f32[32,80,192]{2,1,0:T(8,128)S(1)} %fusion.21, f32[32,80,192]{2,1,0:T(8,128)S(1)} %fusion.22, f32[32,80,192]{2,1,0:T(8,128)S(1)} %fusion.23, f32[32,80,192]{2,1,0:T(8,128)} %fusion.24, f32[32,80,192]{2,1,0:T(8,128)S(1)} %fusion.25, ...), kind=kOutput, calls=%fused_computation.41 | convolution fusion | flops 383874560 | bytes 22768640 | tf_op jit(solution)/shard_map/oi,irw->orw/dot_general | solution.py:38
  274.6 4.6 %collective-permute-start.10 = (bf16[3,192,1,80]{1,3,2,0:T(8,128)(2,1)S(1)}, bf16[3,192,1,80]{1,3,2,0:T(8,128)(2,1)S(1)}, u32[]{:S(2)}, u32[]{:S(2)}) collective-permute-start(bf16[3,192,1,80]{1,3,2,0:T(8,128)(2,1)S(1)} %get-tuple-element.9), channel_id=1, source_target_pairs={{0,8},{8,16},{16,24},{24,32},{32,40},{40,48},{48,56},{56,64},{64,7... | collective-permute-start | bytes 276488 | tf_op jit(solution)/shard_map/ppermute | solution.py:14
  279.2 2.2 collective-permute-start.11
  281.3 2.4 fusion.318
  283.8 3.1 collective-permute-done.11
  287.1 2.2 collective-permute-start.12
  289.3 3.1 collective-permute-start.13
  292.4 2.1 fusion.96
  304.5 6.9 %pad_maximum_fusion = (bf16[3,192,34,81]{1,3,2,0:T(8,128)(2,1)S(1)}, bf16[3,192,34,81]{1,3,2,0:T(8,128)(2,1)S(1)}) fusion(bf16[3,192,34,1]{1,3,2,0:T(2,128)(2,1)S(1)} %collective-permute-done.13, bf16[3,192,1,80]{1,3,2,0:T(8,128)(2,1)S(1)} %collective-permute-done.11, bf16[1,192,32,80]{1,3,2,0:T(8,128)(2,1)S(1)} %fusion.402, ...), kind=kLoop, calls=%fused_computation.1 | loop fusion | flops 31726080 | bytes 9556992 | tf_op jit(solution)/shard_map/concatenate | solution.py:16
  311.4 2.3 fusion.101
  315.7 2.1 fusion.63
  319.8 2.1 fusion.64
  330.0 2.1 fusion.78
  332.0 2.1 fusion.79
  336.2 2.1 fusion.86
  342.3 2.1 fusion.94
  346.7 22.7 %fusion.10 = bf16[192,32,80]{0,2,1:T(8,128)(2,1)} fusion(f32[32,80,192]{2,1,0:T(8,128)} %fusion.58, f32[32,80,192]{2,1,0:T(8,128)} %fusion.61, f32[32,80,192]{2,1,0:T(8,128)} %fusion.62, f32[32,80,192]{2,1,0:T(8,128)} %fusion.318, f32[32,80,192]{2,1,0:T(8,128)} %fusion.63, f32[32,80,192]{2,1,0:T(8,128)} %fusion.64, f32[32,80,192]{2,1,0:T(8,128)} %fusion.66, ...), kind=kOutput, calls=%fused_computation.16 | convolution fusion | flops 203489280 | bytes 70877952 | tf_op jit(solution)/shard_map/oi,irw->orw/dot_general | solution.py:38
  (156 shorter events, 79.2 us)
Async XLA Ops:
  6.5 195.0 %copy-start = (bf16[384,192]{0,1:T(8,128)(2,1)S(1)}, bf16[384,192]{0,1:T(8,128)(2,1)}, u32[]{:S(2)}) copy-start(bf16[384,192]{0,1:T(8,128)(2,1)} %param.30) | copy-start | bytes 442372
  6.5 58.7 %all-gather.2.cloned.1.call-start = ((), (), s32[]{:S(2)}) async-start(), calls=%async_computation | async-start | bytes 5308416 | tf_op jit(solution)/shard_map/all_gather | solution.py:88
  71.9 10.8 %copy-start.2 = (bf16[2,192,32,80]{1,3,2,0:T(8,128)(2,1)S(1)}, bf16[2,192,32,80]{1,3,2,0:T(8,128)(2,1)}, u32[]{:S(2)}) copy-start(bf16[2,192,32,80]{1,3,2,0:T(8,128)(2,1)} %param.34) | copy-start | bytes 5898244
  73.6 21.3 %collective-permute-start = (bf16[3,384,2,160]{1,3,2,0:T(8,128)(2,1)S(1)}, bf16[3,384,2,160]{1,3,2,0:T(8,128)(2,1)S(1)}, u32[]{:S(2)}, u32[]{:S(2)}) collective-permute-start(bf16[3,384,2,160]{1,3,2,0:T(8,128)(2,1)S(1)} %get-tuple-element.11), channel_id=1, source_target_pairs={{0,8},{8,16},{16,24},{24,32},{32,40},{40,48},{48,56},{56,64},{64,7... | collective-permute-start | bytes 2211848 | tf_op jit(solution)/shard_map/ppermute | solution.py:14
  78.6 18.2 %collective-permute-start.1 = (bf16[3,384,2,160]{1,3,2,0:T(8,128)(2,1)S(1)}, bf16[3,384,2,160]{1,3,2,0:T(8,128)(2,1)S(1)}, u32[]{:S(2)}, u32[]{:S(2)}) collective-permute-start(bf16[3,384,2,160]{1,3,2,0:T(8,128)(2,1)S(1)} %get-tuple-element.12), channel_id=1, source_target_pairs={{8,0},{16,8},{24,16},{32,24},{40,32},{48,40},{56,48},{64,56},{72,6... | collective-permute-start | bytes 2211848 | tf_op jit(solution)/shard_map/ppermute | solution.py:15
  82.7 14.0 %copy-start.3 = (bf16[3,384,8,160]{1,3,2,0:T(8,128)(2,1)S(1)}, bf16[3,384,8,160]{1,3,2,0:T(8,128)(2,1)}, u32[]{:S(2)}) copy-start(bf16[3,384,8,160]{1,3,2,0:T(8,128)(2,1)} %copy.23) | copy-start | bytes 8847364
  96.7 3.2 slice-start
  97.4 1.0 copy-start.16
  97.4 2.9 slice-start.1
  100.2 16.7 %copy-start.4 = (bf16[1,384,12,162]{1,3,2,0:T(8,128)(2,1)}, bf16[1,384,12,162]{1,3,2,0:T(8,128)(2,1)S(1)}, u32[]{:S(2)}) copy-start(bf16[1,384,12,162]{1,3,2,0:T(8,128)(2,1)S(1)} %fusion.7) | copy-start | bytes 4478980
  160.3 2.4 copy-start.17
  189.2 2.7 copy-start.14
  193.3 1.2 copy-start.24
  193.7 1.3 copy-start.20
  194.1 1.2 copy-start.5
  194.1 7.4 %copy-start.18 = (f32[384]{0:T(512)S(1)}, f32[384]{0:T(512)}, u32[]{:S(2)}) copy-start(f32[384]{0:T(512)} %param.31) | copy-start | bytes 4612
  195.0 18.0 %copy-start.12 = (bf16[3,3,3,384,192]{3,4,2,1,0:T(8,128)(2,1)S(1)}, bf16[3,3,3,384,192]{3,4,2,1,0:T(8,128)(2,1)}, u32[]{:S(2)}) copy-start(bf16[3,3,3,384,192]{3,4,2,1,0:T(8,128)(2,1)} %param.28) | copy-start | bytes 11943940
  195.3 6.6 %collective-permute-start.2 = (bf16[3,192,1,40]{1,3,2,0:T(8,128)(2,1)S(1)}, bf16[3,192,1,40]{1,3,2,0:T(8,128)(2,1)S(1)}, u32[]{:S(2)}, u32[]{:S(2)}) collective-permute-start(bf16[3,192,1,40]{1,3,2,0:T(8,128)(2,1)S(1)} %get-tuple-element.19), channel_id=1, source_target_pairs={{0,8},{8,16},{16,24},{24,32},{32,40},{40,48},{48,56},{56,64},{64,7... | collective-permute-start | bytes 138248 | tf_op jit(solution)/shard_map/ppermute | solution.py:14
  199.6 7.0 %collective-permute-start.3 = (bf16[3,192,1,40]{1,3,2,0:T(8,128)(2,1)S(1)}, bf16[3,192,1,40]{1,3,2,0:T(8,128)(2,1)S(1)}, u32[]{:S(2)}, u32[]{:S(2)}) collective-permute-start(bf16[3,192,1,40]{1,3,2,0:T(8,128)(2,1)S(1)} %get-tuple-element.20), channel_id=1, source_target_pairs={{8,0},{16,8},{24,16},{32,24},{40,32},{48,40},{56,48},{64,56},{72,6... | collective-permute-start | bytes 138248 | tf_op jit(solution)/shard_map/ppermute | solution.py:15
  206.7 8.3 %collective-permute-start.4 = (bf16[3,192,18,1]{1,3,2,0:T(2,128)(2,1)S(1)}, bf16[3,192,18,1]{1,3,2,0:T(2,128)(2,1)S(1)}, u32[]{:S(2)}, u32[]{:S(2)}) collective-permute-start(bf16[3,192,18,1]{1,3,2,0:T(2,128)(2,1)S(1)} %get-tuple-element.17), channel_id=1, source_target_pairs={{0,1},{1,2},{2,3},{3,4},{4,5},{5,6},{6,7},{8,9},{9,10},{10,11},{11... | collective-permute-start | bytes 62216 | tf_op jit(solution)/shard_map/ppermute | solution.py:14
  211.0 7.0 %collective-permute-start.5 = (bf16[3,192,18,1]{1,3,2,0:T(2,128)(2,1)S(1)}, bf16[3,192,18,1]{1,3,2,0:T(2,128)(2,1)S(1)}, u32[]{:S(2)}, u32[]{:S(2)}) collective-permute-start(bf16[3,192,18,1]{1,3,2,0:T(2,128)(2,1)S(1)} %get-tuple-element.18), channel_id=1, source_target_pairs={{1,0},{2,1},{3,2},{4,3},{5,4},{6,5},{7,6},{9,8},{10,9},{11,10},{12... | collective-permute-start | bytes 62216 | tf_op jit(solution)/shard_map/ppermute | solution.py:15
  223.2 1.2 copy-start.11
  223.6 1.3 copy-start.10
  226.1 0.7 copy-start.19
  226.7 6.5 %copy-start.9 = (bf16[1,192,32,80]{1,3,2,0:T(8,128)(2,1)S(1)}, bf16[1,192,32,80]{1,3,2,0:T(8,128)(2,1)}, u32[]{:S(2)}) copy-start(bf16[1,192,32,80]{1,3,2,0:T(8,128)(2,1)} %get-tuple-element.13) | copy-start | bytes 2949124
  227.3 16.1 %copy-start.8 = (bf16[1,192,32,80]{1,3,2,0:T(8,128)(2,1)S(1)}, bf16[1,192,32,80]{1,3,2,0:T(8,128)(2,1)}, u32[]{:S(2)}) copy-start(bf16[1,192,32,80]{1,3,2,0:T(8,128)(2,1)} %get-tuple-element.14) | copy-start | bytes 2949124
  227.3 8.9 %collective-permute-start.6 = (bf16[384,1,40]{0,2,1:T(8,128)(2,1)S(1)}, bf16[384,1,40]{0,2,1:T(8,128)(2,1)S(1)}, u32[]{:S(2)}, u32[]{:S(2)}) collective-permute-start(bf16[384,1,40]{0,2,1:T(8,128)(2,1)S(1)} %get-tuple-element.25), channel_id=1, source_target_pairs={{0,8},{8,16},{16,24},{24,32},{32,40},{40,48},{48,56},{56,64},{64,7... | collective-permute-start | bytes 92168 | tf_op jit(solution)/shard_map/ppermute | solution.py:14
  231.3 6.7 %collective-permute-start.7 = (bf16[384,1,40]{0,2,1:T(8,128)(2,1)S(1)}, bf16[384,1,40]{0,2,1:T(8,128)(2,1)S(1)}, u32[]{:S(2)}, u32[]{:S(2)}) collective-permute-start(bf16[384,1,40]{0,2,1:T(8,128)(2,1)S(1)} %get-tuple-element.26), channel_id=1, source_target_pairs={{8,0},{16,8},{24,16},{32,24},{40,32},{48,40},{56,48},{64,56},{72,6... | collective-permute-start | bytes 92168 | tf_op jit(solution)/shard_map/ppermute | solution.py:15
  238.1 8.3 %collective-permute-start.8 = (bf16[384,18,1]{0,2,1:T(2,128)(2,1)S(1)}, bf16[384,18,1]{0,2,1:T(2,128)(2,1)S(1)}, u32[]{:S(2)}, u32[]{:S(2)}) collective-permute-start(bf16[384,18,1]{0,2,1:T(2,128)(2,1)S(1)} %get-tuple-element.23), channel_id=1, source_target_pairs={{0,1},{1,2},{2,3},{3,4},{4,5},{5,6},{6,7},{8,9},{9,10},{10,11},{11... | collective-permute-start | bytes 41480 | tf_op jit(solution)/shard_map/ppermute | solution.py:14
  240.0 6.7 %collective-permute-start.9 = (bf16[384,18,1]{0,2,1:T(2,128)(2,1)S(1)}, bf16[384,18,1]{0,2,1:T(2,128)(2,1)S(1)}, u32[]{:S(2)}, u32[]{:S(2)}) collective-permute-start(bf16[384,18,1]{0,2,1:T(2,128)(2,1)S(1)} %get-tuple-element.24), channel_id=1, source_target_pairs={{1,0},{2,1},{3,2},{4,3},{5,4},{6,5},{7,6},{9,8},{10,9},{11,10},{12... | collective-permute-start | bytes 41480 | tf_op jit(solution)/shard_map/ppermute | solution.py:15
  256.1 2.9 copy-start.15
  268.2 0.9 copy-start.21
  269.0 4.6 %copy-start.22 = (f32[192]{0:T(256)S(1)}, f32[192]{0:T(256)}, u32[]{:S(2)}) copy-start(f32[192]{0:T(256)} %param.35) | copy-start | bytes 2308
  274.5 6.8 %copy-start.13 = (bf16[3,3,3,192,192]{4,3,2,1,0:T(8,128)(2,1)S(1)}, bf16[3,3,3,192,192]{4,3,2,1,0:T(8,128)(2,1)}, u32[]{:S(2)}) copy-start(bf16[3,3,3,192,192]{4,3,2,1,0:T(8,128)(2,1)} %param.36) | copy-start | bytes 5971972
  274.6 9.2 %collective-permute-start.10 = (bf16[3,192,1,80]{1,3,2,0:T(8,128)(2,1)S(1)}, bf16[3,192,1,80]{1,3,2,0:T(8,128)(2,1)S(1)}, u32[]{:S(2)}, u32[]{:S(2)}) collective-permute-start(bf16[3,192,1,80]{1,3,2,0:T(8,128)(2,1)S(1)} %get-tuple-element.9), channel_id=1, source_target_pairs={{0,8},{8,16},{16,24},{24,32},{32,40},{40,48},{48,56},{56,64},{64,7... | collective-permute-start | bytes 276488 | tf_op jit(solution)/shard_map/ppermute | solution.py:14
  279.2 7.7 %collective-permute-start.11 = (bf16[3,192,1,80]{1,3,2,0:T(8,128)(2,1)S(1)}, bf16[3,192,1,80]{1,3,2,0:T(8,128)(2,1)S(1)}, u32[]{:S(2)}, u32[]{:S(2)}) collective-permute-start(bf16[3,192,1,80]{1,3,2,0:T(8,128)(2,1)S(1)} %get-tuple-element.10), channel_id=1, source_target_pairs={{8,0},{16,8},{24,16},{32,24},{40,32},{48,40},{56,48},{64,56},{72,6... | collective-permute-start | bytes 276488 | tf_op jit(solution)/shard_map/ppermute | solution.py:15
  287.1 17.4 %collective-permute-start.12 = (bf16[3,192,34,1]{1,3,2,0:T(2,128)(2,1)S(1)}, bf16[3,192,34,1]{1,3,2,0:T(2,128)(2,1)S(1)}, u32[]{:S(2)}, u32[]{:S(2)}) collective-permute-start(bf16[3,192,34,1]{1,3,2,0:T(2,128)(2,1)S(1)} %get-tuple-element.8), channel_id=1, source_target_pairs={{0,1},{1,2},{2,3},{3,4},{4,5},{5,6},{6,7},{8,9},{9,10},{10,11},{11... | collective-permute-start | bytes 117512 | tf_op jit(solution)/shard_map/ppermute | solution.py:14
  289.3 15.2 %collective-permute-start.13 = (bf16[3,192,34,1]{1,3,2,0:T(2,128)(2,1)S(1)}, bf16[3,192,34,1]{1,3,2,0:T(2,128)(2,1)S(1)}, u32[]{:S(2)}, u32[]{:S(2)}) collective-permute-start(bf16[3,192,34,1]{1,3,2,0:T(2,128)(2,1)S(1)} %get-tuple-element.7), channel_id=1, source_target_pairs={{1,0},{2,1},{3,2},{4,3},{5,4},{6,5},{7,6},{9,8},{10,9},{11,10},{12... | collective-permute-start | bytes 117512 | tf_op jit(solution)/shard_map/ppermute | solution.py:15
  311.4 33.0 %copy-start.6 = (bf16[3,192,34,81]{1,3,2,0:T(8,128)(2,1)}, bf16[3,192,34,81]{1,3,2,0:T(8,128)(2,1)S(1)}, u32[]{:S(2)}) copy-start(bf16[3,192,34,81]{1,3,2,0:T(8,128)(2,1)S(1)} %get-tuple-element.5) | copy-start | bytes 9517828
  344.4 2.3 copy-start.7
  344.4 2.3 copy-start.23
  346.7 22.7 %copy-start.1 = (bf16[384,192]{0,1:T(8,128)(2,1)S(1)}, bf16[384,192]{0,1:T(8,128)(2,1)}, u32[]{:S(2)}) copy-start(bf16[384,192]{0,1:T(8,128)(2,1)} %param.30) | copy-start | bytes 442372
Sparse Core Ops, SparseCore 0:
  9.0 56.2 all-gather.1
where the time goes:
time: 383 us; the launch traced here: 377 us
  matrix products  197 us (51%)
  waiting for transfers between devices  78.6 us (21%)
  starting transfers between devices  42.6 us (11%)
  local copies, waits for them, and re-layouts  27.7 us (7%)
  other arithmetic  15.9 us (4%)
  between operations  14.7 us (4%)
    dot_general x95, matrix products, convolve(): jnp.einsum('oi,irw->orw', kernel[frame_index, row_tap, col_tap], piece, p...  187 us
    all_gather x1, waiting for transfers between devices, per_device(): gathered = lax.all_gather(stacked, 'wa', axis=1, tiled=True)  53.3 us
    ppermute x7, starting transfers between devices, padded(): before = lax.ppermute(last, axis, up)  26.3 us
    ppermute x7, starting transfers between devices, padded(): after = lax.ppermute(leading, axis, down)  16.3 us
    ppermute x7, waiting for transfers between devices, padded(): after = lax.ppermute(leading, axis, down)  14.9 us
    ppermute x7, waiting for transfers between devices, padded(): before = lax.ppermute(last, axis, up)  10.5 us
    unnamed x4, matrix products  10.3 us
    concatenate x5, other arithmetic, padded(): x = jnp.concatenate([before, x, after], axis=dim)  9.18 us
  transfers between devices with their start and end apart: 15, of which 8 were waited for; matrix products, arithmetic and copies ran while one was open for 8% of the time, Pallas kernels for 0%

commit v1 on v0

v1 whole, which is shorter than its diff:
```python
import jax
import jax.numpy as jnp
from jax import lax
from jax.experimental import pallas as pl
from jax.experimental.pallas import tpu as pltpu
from jax.sharding import PartitionSpec as P

BF = jnp.bfloat16
F32 = jnp.float32
MESH = pl.DeviceIdType.MESH
NA, NW = 16, 8
EPS = 1e-06
NT = (((1,), (1,)), ((), ()))


def act(v, g, channels):
    ms = jnp.sum(v * v, axis=1, keepdims=True) * (1.0 / channels)
    u = v * lax.rsqrt(ms + EPS) * g
    return 0.5 * u * (1.0 + jnp.tanh(0.5 * u))


def nt_dot(x, w):
    return lax.dot_general(x, w, NT, preferred_element_type=F32)


def fold_weights(raw, out):
    def chunk(src, first, step):
        k = [[raw[a, b, pl.ds(src, 16), :].astype(F32) for b in range(3)] for a in range(3)]
        rowed = [[[k[0][b] + k[1][b] for b in range(3)], k[2]],
                 [k[0], [k[1][b] + k[2][b] for b in range(3)]]]
        for sr in range(2):
            for sc in range(2):
                at = first + (sr * 2 + sc) * step
                for ta in range(2):
                    r = rowed[sr][ta]
                    cols = [r[0] + r[1], r[2]] if sc == 0 else [r[0], r[1] + r[2]]
                    for tb in range(2):
                        lane = (ta * 2 + tb) * 384
                        out[pl.ds(at, 16), lane : lane + 384] = cols[tb].astype(BF)

    for c in range(8):
        chunk(c * 16, c * 16, 128)
    for c in range(4):
        chunk(128 + c * 16, 512 + c * 16, 64)


def put_phases(block, bias, img, row, first):
    n = block.shape[0]
    lo, hi = bias[:, 0:128], bias[:, 128:192]
    for s in range(4):
        at = pl.ds(first + s % 2, n, stride=2)
        img[0, row + s // 2, at, :] = block[:, s * 128 : s * 128 + 128] + lo
        high = block[:, 512 + s * 64 : 576 + s * 64] + hi
        img[1, row + s // 2, at, :] = jnp.concatenate([high, jnp.zeros((n, 64), F32)], 1)


def image_row(img, row, cols):
    return jnp.concatenate([img[0, row, cols, :], img[1, row, cols, 0:64]], -1)


def pack_fine(raw, cached, current):
    n = cached.shape[0]
    for a in range(3):
        c = a * 1152
        for t in range(2):
            for b in range(3):
                i = t * 3 + b
                cached[:, c + i * 128 : c + i * 128 + 128] = raw[t, a, b, :, 0:128]
        for i in range(3):
            p, q = 2 * i, 2 * i + 1
            cached[:, c + 768 + i * 128 : c + 896 + i * 128] = jnp.concatenate(
                [raw[p // 3, a, p % 3, :, 128:192], raw[q // 3, a, q % 3, :, 128:192]], 1)
        c = a * 640
        for b in range(3):
            current[:, c + b * 128 : c + b * 128 + 128] = raw[2, a, b, :, 0:128]
        current[:, c + 384 : c + 512] = jnp.concatenate([raw[2, a, 0, :, 128:192], raw[2, a, 1, :, 128:192]], 1)
        current[:, c + 512 : c + 640] = jnp.concatenate([raw[2, a, 2, :, 128:192], jnp.zeros((n, 64), BF)], 1)


def put_cached(x, at, n, buf, first):
    v = [buf[i // 3, first + i % 3 : first + i % 3 + n, :].astype(BF) for i in range(6)]
    rows = pl.ds(at, n)
    for i in range(6):
        x[rows, i * 128 : i * 128 + 128] = v[i][:, 0:128]
    for i in range(3):
        x[rows, 768 + i * 128 : 896 + i * 128] = jnp.concatenate(
            [v[2 * i][:, 128:192], v[2 * i + 1][:, 128:192]], 1)


def put_current(x, at, n, buf, first):
    v = [buf[first + b : first + b + n, :].astype(BF) for b in range(3)]
    rows = pl.ds(at, n)
    for b in range(3):
        x[rows, b * 128 : b * 128 + 128] = v[b][:, 0:128]
    x[rows, 384:512] = jnp.concatenate([v[0][:, 128:192], v[1][:, 128:192]], 1)
    x[rows, 512:640] = jnp.concatenate([v[2][:, 128:192], jnp.zeros((n, 64), BF)], 1)


def taps(x, at, n, pitch):
    return jnp.concatenate([x[pl.ds(at + r * pitch, n), :] for r in range(3)], 1)


def kernel(
    lat, cc, g_c, b_c, b_u, g_m, b_m, b_b, b_n, g_f, b_f, ft, mt, ck, uk, mk, bk, nk, fk,
    out,
    v_coarse, v_f, v_m, v_g, v_ck, v_uk, v_mf, v_mh, v_bk, v_nk, v_fk,
    s0, s1, e32, edge, pack, wfc, wf2, w4u, w4n, xfc, xf2, xmc, xm2,
    img_c, img_l, img1, img_m, img2, img_f, rb_f, rb_m, rb_1, g32,
    lf, rf, lm, rm, acc_f, acc_m, sem, osem, send, recv,
):
    a = lax.axis_index("ha")
    w = lax.axis_index("wa")
    north, south = a > 0, a < NA - 1
    west, east = w > 0, w < NW - 1
    barrier = pltpu.get_barrier_semaphore()

    def greet(da, k):
        pl.semaphore_signal(
            barrier, inc=1, device_id=(a + da, lax.rem(w + k, NW)), device_id_type=MESH
        )

    for k in range(1, NW):
        greet(0, k)

    @pl.when(north)
    def _():
        for k in range(NW):
            greet(-1, k)

    @pl.when(south)
    def _():
        for k in range(NW):
            greet(1, k)

    count = [0]

    def load(src, dst):
        c = pltpu.make_async_copy(src, dst, sem.at[count[0]])
        count[0] += 1
        c.start()
        return c

    d_m = load(mt, v_m.at[:, pl.ds(2, 16)])
    d_f = load(ft, v_f.at[:, pl.ds(1, 32)])
    d_uk = load(uk, v_uk)
    d_nk = load(nk, v_nk)
    d_fk = load(fk, v_fk)
    d_mf = load(mk.at[:, :, :, pl.ds(0, 128), :], v_mf)
    d_mh = load(mk.at[:, :, :, pl.ds(128, 64), :], v_mh)
    d_bk = load(bk, v_bk)
    d_ck = [load(ck.at[t], v_ck.at[t]) for t in range(3)]

    def column(ref, t, first, n, tile, col):
        x = ref[t, first : first + n, tile : tile + 8, :].astype(F32)
        s0[0:n] = x[:, :, 0:128]
        s1[0:n] = jnp.concatenate([x[:, :, 128:192], jnp.zeros((n, 8, 64), F32)], 2)
        return [jnp.concatenate([s0[0:n, c, :], s1[0:n, c, 0:64]], 1) for c in col]

    d_m.wait()
    d_f.wait()
    e32[:, 128:192, :] = jnp.zeros((2, 64, 192), F32)
    for t in range(2):
        for side in range(2):
            (f,) = column(v_f, t, 1, 32, 72 - 72 * side, (7 - 7 * side,))
            m = column(v_m, t, 2, 16, 32 - 32 * side, (6 - 6 * side, 7 - 6 * side))
            e32[t, 64 * side : 64 * side + 32, :] = f
            e32[t, 64 * side + 32 : 64 * side + 48, :] = m[0]
            e32[t, 64 * side + 48 : 64 * side + 64, :] = m[1]
            for north_end in range(2):
                at = 128 + 32 * north_end + 16 * side
                h, r = 31 - 31 * north_end, 14 - 14 * north_end
                e32[t, at : at + 1, :] = f[h : h + 1]
                e32[t, at + 1 : at + 3, :] = m[0][r : r + 2]
                e32[t, at + 3 : at + 5, :] = m[1][r : r + 2]
    edge[...] = e32[...].astype(BF)

    quarter = lax.broadcasted_iota(jnp.int32, (1, 128), 1) // 32
    for t in range(3):
        x = (lat[...] if t == 2 else cc[t]).astype(F32)
        s0[...] = x[:, :, 0:128]
        s1[...] = jnp.concatenate([x[:, :, 128:160], jnp.zeros((48, 8, 96), F32)], 2)
        for half in range(2):
            rows4 = [jnp.concatenate([s0[:, half * 4 + h, :], s1[:, half * 4 + h, :]], 1) for h in range(4)]
            for to in range(NW):
                got = None
                for h in range(4):
                    shift = (half * 128 + h * 32 - (20 * to - 3)) % 256
                    moved = pltpu.roll(rows4[h], shift, 1)[:, half * 128 : half * 128 + 128]
                    got = moved if got is None else jnp.where(quarter == h, moved, got)
                pack[to, t, :, half * 128 : half * 128 + 128] = got.astype(BF)

    pl.semaphore_wait(barrier, NW - 1 + NW * (jnp.where(north, 1, 0) + jnp.where(south, 1, 0)))

    mine = pl.ds(pl.multiple_of(w * 48, 16), 48)
    copies = []

    def remote(src, dst, da, to_w, cond_send, cond_recv):
        s = len(copies)
        c = pltpu.make_async_remote_copy(
            src_ref=src, dst_ref=dst, send_sem=send.at[s], recv_sem=recv.at[s],
            device_id=(a + da, to_w), device_id_type=MESH)
        copies.append((c, cond_send, cond_recv))

    remote(edge.at[:, pl.ds(0, 64)], v_g.at[:, pl.ds(0, 64)], 0, w + 1, east, west)
    remote(edge.at[:, pl.ds(64, 64)], v_g.at[:, pl.ds(64, 64)], 0, w - 1, west, east)
    for i, (da, dw) in enumerate(((1, 1), (1, -1), (-1, 1), (-1, -1))):
        go_a, from_a = (south, north) if da == 1 else (north, south)
        go_w, from_w = (east, west) if dw == 1 else (west, east)
        strip = pl.ds(128 + 16 * i, 16)
        remote(edge.at[:, strip], v_g.at[:, strip], da, w + dw,
               jnp.logical_and(go_a, go_w), jnp.logical_and(from_a, from_w))
    n_edge = len(copies)
    remote(mt.at[:, pl.ds(14, 2)], v_m.at[:, pl.ds(0, 2)], 1, w, south, north)
    remote(mt.at[:, pl.ds(0, 2)], v_m.at[:, pl.ds(18, 2)], -1, w, north, south)
    n_mid = len(copies)
    remote(ft.at[:, 31], v_f.at[:, 0], 1, w, south, north)
    remote(ft.at[:, 0], v_f.at[:, 33], -1, w, north, south)
    n_fine = len(copies)
    for k in range(1, NW):
        to = lax.rem(w + k, NW)
        remote(pack.at[to], v_coarse.at[:, mine, pl.ds(128, 256)], 0, to, None, None)
    for k in range(NW):
        to = lax.rem(w + k, NW)
        remote(pack.at[to, :, :, pl.ds(128, 128)], v_coarse.at[:, mine, pl.ds(0, 128)], 1, to, south, north)
        remote(pack.at[to, :, :, pl.ds(0, 128)], v_coarse.at[:, mine, pl.ds(384, 128)], -1, to, north, south)
    for c, cs, _ in copies:
        if cs is None:
            c.start()
        else:
            pl.when(cs)(c.start)

    def arrived(first, last):
        for c, _, cr in copies[first:last]:
            if cr is None:
                c.wait_recv()
            else:
                pl.when(cr)(c.wait_recv)

    v_coarse[:, mine, 128:384] = pack[w]
    cgain, cbias, ubias, mgain, mbias, bbias, nbias, fgain, fbias = [
        v[...].reshape(1, -1) for v in (g_c, b_c, b_u, g_m, b_m, b_b, b_n, g_f, b_f)]
    mbias = mbias + bbias

    img1[...] = jnp.zeros_like(img1)
    rb_m[...] = jnp.zeros_like(rb_m)
    rb_1[...] = jnp.zeros_like(rb_1)
    img_m[...] = jnp.zeros_like(img_m)

    d_uk.wait()
    d_nk.wait()
    d_fk.wait()
    d_mf.wait()
    d_mh.wait()
    d_bk.wait()

    arrived(0, n_fine)
    no_n, no_s, no_w, no_e = a == 0, a == NA - 1, w == 0, w == NW - 1

    @pl.when(no_n)
    def _():
        v_m[:, 0:2] = jnp.zeros((2, 2, 40, 192), BF)
        v_f[:, 0:1] = jnp.zeros((2, 1, 80, 192), BF)

    @pl.when(no_s)
    def _():
        v_m[:, 18:20] = jnp.zeros((2, 2, 40, 192), BF)
        v_f[:, 33:34] = jnp.zeros((2, 1, 80, 192), BF)

    spans = ((0, 64, no_w), (64, 128, no_e), (128, 144, no_n | no_w), (144, 160, no_n | no_e),
             (160, 176, no_s | no_w), (176, 192, no_s | no_e))
    for lo, hi, gone in spans:
        g32[:, lo:hi, :] = jnp.where(gone, 0.0, v_g[:, lo:hi, :].astype(F32))
    for t in range(2):
        for l, m, base, n, s in ((lf, lm, 0, 128, 160), (rf, rm, 64, 144, 176)):
            l[t, 0:1, :] = g32[t, n : n + 1, :]
            l[t, 1:33, :] = g32[t, base : base + 32, :]
            l[t, 33:34, :] = g32[t, s : s + 1, :]
            for c in range(2):
                m[t, c, 0:2, :] = g32[t, n + 1 + 2 * c : n + 3 + 2 * c, :]
                m[t, c, 2:18, :] = g32[t, base + 32 + 16 * c : base + 48 + 16 * c, :]
                m[t, c, 18:20, :] = g32[t, s + 1 + 2 * c : s + 3 + 2 * c, :]

    for r in range(20):
        buf = rb_m.at[r % 2]
        for t in range(2):
            buf[t, 8:48, :] = v_m[t, r].astype(F32)
            for c in range(2):
                buf[t, 6 + c : 7 + c, :] = lm[t, c, r : r + 1, :]
                buf[t, 48 + c : 49 + c, :] = rm[t, c, r : r + 1, :]
        put_cached(xmc, r * 48, 48, buf, 6)

    def mid_part(i):
        at = i * 288
        k = jnp.concatenate(
            [v[t, r, b] for r in range(3) for v in (v_mf, v_mh) for t in range(2) for b in range(3)], 0)
        acc_m[pl.ds(at, 288), :] = jnp.dot(taps(xmc, at, 288, 48), k, preferred_element_type=F32) + mbias

    for i in range(3):
        mid_part(i)
    fold_weights(v_uk, w4u)
    fold_weights(v_nk, w4n)
    pack_fine(v_fk, wfc, wf2)

    def fine_cached(r):
        buf = rb_f.at[r % 2]
        for t in range(2):
            buf[t, 8:88, :] = v_f[t, r].astype(F32)
            buf[t, 7:8, :] = lf[t, r : r + 1, :]
            buf[t, 88:89, :] = rf[t, r : r + 1, :]
        put_cached(xfc, r * 80, 80, buf, 7)

    for i in range(4):
        for r in range(8 * i + 2 if i else 0, 8 * i + 10):
            fine_cached(r)
        acc_f[i * 640 : i * 640 + 640, :] = nt_dot(taps(xfc, i * 640, 640, 80), wfc[...]) + fbias

    arrived(n_fine, len(copies))
    for t in range(3):
        d_ck[t].wait()
    lane = lax.broadcasted_iota(jnp.int32, (1, 512), 1)
    keep = jnp.logical_and(jnp.logical_or(lane >= 128, a > 0), jnp.logical_or(lane < 384, a < NA - 1))
    for t in range(3):
        for p in range(4):
            part = jnp.where(keep[:, p * 128 : p * 128 + 128],
                             v_coarse[t, :, p * 128 : p * 128 + 128].astype(F32), 0.0)
            flat = part.T
            if t == 2:
                img_l[p * 4 : p * 4 + 4] = flat.reshape(4, 32, 384)
                flat = act(flat, cgain, 384)
            img_c[p * 4 : p * 4 + 4, 0:32, :] = flat.reshape(4, 32, 384)
        for b in range(3):
            v = img_c[1:15, b : b + 24, :].reshape(336, 384)
            for ra in range(3):
                at = (t * 3 + ra) * 288
                xfc[at : at + 288, b * 384 : b * 384 + 384] = v[ra * 24 : ra * 24 + 288].astype(BF)
    total = img_l[2:14, 1:25, :].reshape(288, 384) + cbias
    for t in range(3):
        x = jnp.concatenate([xfc[(t * 3 + ra) * 288 : (t * 3 + ra + 1) * 288, :] for ra in range(3)], 1)
        k = jnp.concatenate([v_ck[t, ra, b] for ra in range(3) for b in range(3)], 1)
        total = total + nt_dot(x, k)
    rid = lax.broadcasted_iota(jnp.int32, (12, 24, 1), 0) + (a * 8 - 2)
    cid = lax.broadcasted_iota(jnp.int32, (12, 24, 1), 1) + (w * 20 - 2)
    inside = (rid >= 0) & (rid < 128) & (cid >= 0) & (cid < 160)
    img1[:, 0:24, :] = jnp.where(inside, total.reshape(12, 24, 384), 0.0)
    for b in range(2):
        xmc[0:384, b * 384 : b * 384 + 384] = img1[:, b : b + 32, :].reshape(384, 384).astype(BF)

    x = jnp.concatenate([xmc[0:352, 0:768], xmc[32:384, 0:768]], 1)
    u = nt_dot(x, w4u[...])
    for i in range(11):
        put_phases(u[i * 32 : i * 32 + 32, :], ubias, img_m, 2 * i, 5)

    mcol = lax.broadcasted_iota(jnp.int32, (72, 1), 0) + (w * 40 - 8)
    mcol = jnp.where((mcol >= 0) & (mcol < 320), 1.0, 0.0)

    def mid_row(r):
        row = a * 16 - 2 + r
        ok = jnp.where((row >= 0) & (row < 256), 1.0, 0.0)
        buf = rb_1.at[r % 4]
        buf[0:72, :] = act(image_row(img_m, r + 1, slice(0, 72)), mgain, 192) * (mcol * ok)
        put_current(xm2, r * 48, 48, buf, 6)

    def bypass_row(r):
        xmc[r * 48 : r * 48 + 48, 768:960] = image_row(img_m, r + 2, slice(7, 55)).astype(BF)

    def mid_block(i):
        at = i * 288
        zero = jnp.zeros((64, 384), BF)
        k = jnp.concatenate(
            [p for r in range(3) for p in
             [v_mf[2, r, b] for b in range(3)] + [v_mh[2, r, b] for b in range(3)] + [zero]], 0)
        total = (acc_m[pl.ds(at, 288), :]
                 + jnp.dot(xmc[pl.ds(at, 288), 768:960], v_bk[...], preferred_element_type=F32)
                 + jnp.dot(taps(xm2, at, 288, 48), k, preferred_element_type=F32))
        rid = lax.broadcasted_iota(jnp.int32, (6, 48, 1), 0) + (a * 16 - 1 + i * 6)
        cid = lax.broadcasted_iota(jnp.int32, (6, 48, 1), 1) + (w * 40 - 1)
        inside = (rid >= 0) & (rid < 256) & (cid >= 0) & (cid < 320)
        img2[i * 6 : i * 6 + 6, 0:48, :] = jnp.where(inside, total.reshape(6, 48, 384), 0.0)
        for r in range(i * 6, i * 6 + 6):
            for b in range(2):
                xmc[r * 48 : r * 48 + 48, b * 384 : b * 384 + 384] = img2[r, b : b + 48, :].astype(BF)

    xmc[864:912, 0:768] = jnp.zeros((48, 768), BF)
    for i in range(3):
        for r in range(6 * i + 2 if i else 0, 6 * i + 8):
            mid_row(r)
        for r in range(6 * i, 6 * i + 6):
            bypass_row(r)
        mid_block(i)

    def fine_block(i):
        at = i * 288
        x = jnp.concatenate([xmc[at : at + 288, 0:768], xmc[at + 48 : at + 336, 0:768]], 1)
        u = nt_dot(x, w4n[...])
        for j in range(6):
            put_phases(u[j * 48 : j * 48 + 48, :], nbias, img_f, i * 12 + 2 * j, 7)

    fcol = lax.broadcasted_iota(jnp.int32, (96, 1), 0) + (w * 80 - 8)
    fcol = jnp.where((fcol >= 0) & (fcol < 640), 1.0, 0.0)

    def fine_rows(first, last):
        for r in range(first, last):
            row = a * 32 - 1 + r
            ok = jnp.where((row >= 0) & (row < 512), 1.0, 0.0)
            buf = rb_1.at[r % 4]
            buf[0:96, :] = act(image_row(img_f, r, slice(0, 96)), fgain, 192) * (fcol * ok)
            put_current(xf2, r * 80, 80, buf, 7)

    def out_block(i):
        at = i * 640
        total = (image_row(img_f, slice(1 + i * 8, 9 + i * 8), slice(8, 88)).reshape(640, 192)
                 + acc_f[at : at + 640, :] + nt_dot(taps(xf2, at, 640, 80), wf2[...]))
        v_f[0, i * 8 : i * 8 + 8] = total.reshape(8, 80, 192).astype(BF)

    fine_block(0)
    fine_block(1)
    fine_rows(0, 12)
    fine_block(2)
    out_block(0)
    fine_rows(12, 24)
    out_block(1)
    fine_rows(24, 34)
    out_block(2)
    out_block(3)
    done = pltpu.make_async_copy(v_f.at[0, pl.ds(0, 32)], out, osem)
    done.start()
    for c, cs, _ in copies:
        if cs is None:
            c.wait_send()
        else:
            pl.when(cs)(c.wait_send)
    done.wait()


def call(*args):
    anywhere = pl.BlockSpec(memory_space=pl.ANY)
    vmem = pl.BlockSpec(memory_space=pltpu.VMEM)
    V = pltpu.VMEM
    n = 10 + 7 + 16
    return pl.pallas_call(
        kernel,
        out_shape=jax.ShapeDtypeStruct((32, 80, 192), BF),
        in_specs=[vmem] * 11 + [anywhere] * 8,
        out_specs=anywhere,
        scratch_shapes=[
            V((3, 384, 512), BF), V((2, 34, 80, 192), BF), V((2, 20, 40, 192), BF), V((2, 192, 192), BF),
            V((3, 3, 3, 384, 384), BF), V((3, 3, 192, 384), BF),
            V((3, 3, 3, 128, 384), BF), V((3, 3, 3, 64, 384), BF),
            V((192, 384), BF), V((3, 3, 192, 384), BF), V((3, 3, 3, 192, 192), BF),
            V((48, 8, 128), F32), V((48, 8, 128), F32), V((2, 192, 192), F32), V((2, 192, 192), BF), V((8, 3, 48, 256), BF),
            V((192, 3456), BF), V((192, 1920), BF), V((768, 1536), BF), V((768, 1536), BF),
            V((2720, 1152), BF), V((2720, 640), BF), V((960, 1152), BF), V((960, 640), BF),
            V((16, 40, 384), F32), V((16, 32, 384), F32), V((12, 40, 384), F32), V((2, 22, 72, 128), F32),
            V((18, 56, 384), F32), V((2, 36, 104, 128), F32), V((2, 2, 96, 192), F32), V((2, 2, 72, 192), F32),
            V((4, 96, 192), F32), V((2, 192, 192), F32),
            V((2, 40, 192), F32), V((2, 40, 192), F32), V((2, 2, 24, 192), F32), V((2, 2, 24, 192), F32),
            V((2560, 192), F32), V((864, 384), F32),
            pltpu.SemaphoreType.DMA((16,)), pltpu.SemaphoreType.DMA,
            pltpu.SemaphoreType.DMA((n,)), pltpu.SemaphoreType.DMA((n,)),
        ],
        compiler_params=pltpu.CompilerParams(
            collective_id=0, has_side_effects=True, vmem_limit_bytes=63 * 2**20),
    )(*args)


def per_device(
    latent_map, coarse_cache, coarse_gain, coarse_kernel, coarse_bias, upper_kernel, upper_bias,
    middle_cache, middle_gain, middle_kernel, middle_bias, bypass_weight, bypass_bias,
    finer_kernel, finer_bias, fine_cache, fine_gain, fine_kernel, fine_bias,
):
    ft = jnp.transpose(fine_cache, (0, 2, 3, 1))
    mt = jnp.transpose(middle_cache, (0, 2, 3, 1))
    y = call(
        latent_map, coarse_cache, coarse_gain, coarse_bias, upper_bias, middle_gain, middle_bias, bypass_bias,
        finer_bias, fine_gain, fine_bias, ft, mt, coarse_kernel, upper_kernel,
        jnp.transpose(middle_kernel, (0, 1, 2, 4, 3)), bypass_weight.T, finer_kernel, fine_kernel)
    return jnp.transpose(y, (2, 0, 1))


def solution(mesh):
    high = (P("wa", "ha", None), P(None, "wa", "ha", None))
    low = P(None, None, "ha", "wa")
    placed = high + (P(),) * 5 + (low,) + (P(),) * 7 + (low,) + (P(),) * 3
    return jax.shard_map(
        per_device, mesh=mesh, in_specs=placed, out_specs=P(None, "ha", "wa"), check_vma=False
    )
```

time: 383 us -> 49.2 us (0.13); the launches traced: 377 us -> 49.1 us
  matrix products: 197 us -> 0 us
  waiting for transfers between devices: 78.6 us -> 0 us
  Pallas kernels: 0 us -> 46.6 us
  starting transfers between devices: 42.6 us -> 0 us
  local copies, waits for them, and re-layouts: 27.7 us -> 2.46 us
  other arithmetic: 15.9 us -> 0 us
  between operations: 14.7 us -> 0.01 us
    dot_general x96 -> x0, matrix products: 187 us -> none  [the longest x95 187 us: convolve(): jnp.einsum('oi,irw->orw', kernel[frame_index, row_tap, col_tap], piece, p...]
    all_gather x1 -> x0, waiting for transfers between devices: 53.3 us -> none  [per_device(): gathered = lax.all_gather(stacked, 'wa', axis=1, tiled=True)]
    pallas_call x0 -> x1, Pallas kernels: none -> 46.6 us  [call(): pl.pallas_call(kernel, out_shape=jax.ShapeDtypeStruct((32, 80, 192), BF),...]
    ppermute x14 -> x0, starting transfers between devices: 42.6 us -> none  [the longest x7 26.3 us: padded(): before = lax.ppermute(last, axis, up)]
    ppermute x14 -> x0, waiting for transfers between devices: 25.3 us -> none  [the longest x7 14.9 us: padded(): after = lax.ppermute(leading, axis, down)]
    concatenate x6 -> x0, other arithmetic: 11.2 us -> none  [the longest x5 9.18 us: padded(): x = jnp.concatenate([before, x, after], axis=dim)]
    unnamed x4 -> x0, matrix products: 10.3 us -> none
    reshape x2 -> x0, local copies, waits for them, and re-layouts: 7.44 us -> none  [enlarge(): return jnp.repeat(jnp.repeat(values, 2, axis=1), 2, axis=2)]
  transfers between devices with their start and end apart: 15 -> 0, of which waited for: 8 -> 0; matrix products, arithmetic and copies ran while one was open for 8% -> 0% of each run, Pallas kernels for 0% -> 0%
where the time goes in v1:
time: 49.2 us; the launch traced here: 49.1 us
  Pallas kernels  46.6 us (95%)
  local copies, waits for them, and re-layouts  2.46 us (5%)
    pallas_call x1, Pallas kernels, call(): pl.pallas_call(kernel, out_shape=jax.ShapeDtypeStruct((32, 80, 192), BF),...  46.6 us
    unnamed x1, local copies, waits for them, and re-layouts  2.46 us

profile of v1, /device:TPU:99, one launch (start us, length us, event | category | flops | bytes accessed | tf_op | source)
XLA Modules:
  0.0 49.1 jit_solution(11694158330550846172)
XLA Ops:
  0.0 46.6 %shard_map.181 = bf16[32,80,192]{2,1,0:T(8,128)(2,1)} custom-call(bf16[48,8,160]{2,1,0:T(8,128)(2,1)} %lat.1, bf16[2,48,8,160]{3,2,1,0:T(8,128)(2,1)} %cc.1, f32[384]{0:T(512)} %g_c.1, f32[384]{0:T(512)} %b_c.1, f32[192]{0:T(256)} %b_u.1, f32[192]{0:T(256)} %g_m.1, f32[384]{0:T(512)} %b_m.1, f32[384]{0:T(512)} %b_b.1, f32[192]{0:T(256)} %b_n.1, f32[192]{0:T(256)} %g_f.1, ...), custom_call_target="tpu_custom_call" | custom-call | tf_op jit(solution)/shard_map/pallas_call | solution.py:440
  46.6 2.5 %copy.21 = bf16[192,32,80]{0,2,1:T(8,128)(2,1)} copy(bf16[192,32,80]{0,2,1:T(8,128)(2,1)} %bitcast.5) | data formatting | bytes 1966080

commit v2 on v1

--- a/solution.py
+++ b/solution.py
@@ -70,11 +70,12 @@
             p, q = 2 * i, 2 * i + 1
             cached[:, c + 768 + i * 128 : c + 896 + i * 128] = jnp.concatenate(
                 [raw[p // 3, a, p % 3, :, 128:192], raw[q // 3, a, q % 3, :, 128:192]], 1)
-        c = a * 640
+        c = a * 512
         for b in range(3):
             current[:, c + b * 128 : c + b * 128 + 128] = raw[2, a, b, :, 0:128]
         current[:, c + 384 : c + 512] = jnp.concatenate([raw[2, a, 0, :, 128:192], raw[2, a, 1, :, 128:192]], 1)
-        current[:, c + 512 : c + 640] = jnp.concatenate([raw[2, a, 2, :, 128:192], jnp.zeros((n, 64), BF)], 1)
+    current[:, 1536:1664] = jnp.concatenate([raw[2, 0, 2, :, 128:192], raw[2, 1, 2, :, 128:192]], 1)
+    current[:, 1664:1792] = jnp.concatenate([raw[2, 2, 2, :, 128:192], jnp.zeros((n, 64), BF)], 1)
 
 
 def put_cached(x, at, n, buf, first):
@@ -87,13 +88,15 @@
             [v[2 * i][:, 128:192], v[2 * i + 1][:, 128:192]], 1)
 
 
-def put_current(x, at, n, buf, first):
+def put_current(x, xh, r, rows, n, buf, first):
     v = [buf[first + b : first + b + n, :].astype(BF) for b in range(3)]
-    rows = pl.ds(at, n)
+    at = slice(r * n, r * n + n)
     for b in range(3):
-        x[rows, b * 128 : b * 128 + 128] = v[b][:, 0:128]
-    x[rows, 384:512] = jnp.concatenate([v[0][:, 128:192], v[1][:, 128:192]], 1)
-    x[rows, 512:640] = jnp.concatenate([v[2][:, 128:192], jnp.zeros((n, 64), BF)], 1)
+        x[at, b * 128 : b * 128 + 128] = v[b][:, 0:128]
+    x[at, 384:512] = jnp.concatenate([v[0][:, 128:192], v[1][:, 128:192]], 1)
+    for tap in range(3):
+        if 0 <= r - tap < rows:
+            xh[(r - tap) * n : (r - tap) * n + n, tap * 64 : tap * 64 + 64] = v[2][:, 128:192]
 
 
 def taps(x, at, n, pitch):
@@ -104,7 +107,7 @@
     lat, cc, g_c, b_c, b_u, g_m, b_m, b_b, b_n, g_f, b_f, ft, mt, ck, uk, mk, bk, nk, fk,
     out,
     v_coarse, v_f, v_m, v_g, v_ck, v_uk, v_mf, v_mh, v_bk, v_nk, v_fk,
-    s0, s1, e32, edge, pack, wfc, wf2, w4u, w4n, xfc, xf2, xmc, xm2,
+    s0, s1, e32, edge, pack, wfc, wf2, w4u, w4n, xfc, xf2, xfh, xmc, xm2, xmh,
     img_c, img_l, img1, img_m, img2, img_f, rb_f, rb_m, rb_1, g32,
     lf, rf, lm, rm, acc_f, acc_m, sem, osem, send, recv,
 ):
@@ -119,19 +122,6 @@
             barrier, inc=1, device_id=(a + da, lax.rem(w + k, NW)), device_id_type=MESH
         )
 
-    for k in range(1, NW):
-        greet(0, k)
-
-    @pl.when(north)
-    def _():
-        for k in range(NW):
-            greet(-1, k)
-
-    @pl.when(south)
-    def _():
-        for k in range(NW):
-            greet(1, k)
-
     count = [0]
 
     def load(src, dst):
@@ -142,13 +132,34 @@
 
     d_m = load(mt, v_m.at[:, pl.ds(2, 16)])
     d_f = load(ft, v_f.at[:, pl.ds(1, 32)])
-    d_uk = load(uk, v_uk)
-    d_nk = load(nk, v_nk)
-    d_fk = load(fk, v_fk)
-    d_mf = load(mk.at[:, :, :, pl.ds(0, 128), :], v_mf)
-    d_mh = load(mk.at[:, :, :, pl.ds(128, 64), :], v_mh)
-    d_bk = load(bk, v_bk)
-    d_ck = [load(ck.at[t], v_ck.at[t]) for t in range(3)]
+
+    for k in range(1, NW):
+        greet(0, k)
+
+    @pl.when(north)
+    def _():
+        for k in range(NW):
+            greet(-1, k)
+
+    @pl.when(south)
+    def _():
+        for k in range(NW):
+            greet(1, k)
+
+    quarter = lax.broadcasted_iota(jnp.int32, (1, 128), 1) // 32
+    for t in range(3):
+        x = (lat[...] if t == 2 else cc[t]).astype(F32)
+        s0[...] = x[:, :, 0:128]
+        s1[...] = jnp.concatenate([x[:, :, 128:160], jnp.zeros((48, 8, 96), F32)], 2)
+        for half in range(2):
+            rows4 = [jnp.concatenate([s0[:, half * 4 + h, :], s1[:, half * 4 + h, :]], 1) for h in range(4)]
+            for to in range(NW):
+                got = None
+                for h in range(4):
+                    shift = (half * 128 + h * 32 - (20 * to - 3)) % 256
+                    moved = pltpu.roll(rows4[h], shift, 1)[:, half * 128 : half * 128 + 128]
+                    got = moved if got is None else jnp.where(quarter == h, moved, got)
+                pack[to, t, :, half * 128 : half * 128 + 128] = got.astype(BF)
 
     def column(ref, t, first, n, tile, col):
         x = ref[t, first : first + n, tile : tile + 8, :].astype(F32)
@@ -174,21 +185,6 @@
                 e32[t, at + 3 : at + 5, :] = m[1][r : r + 2]
     edge[...] = e32[...].astype(BF)
 
-    quarter = lax.broadcasted_iota(jnp.int32, (1, 128), 1) // 32
-    for t in range(3):
-        x = (lat[...] if t == 2 else cc[t]).astype(F32)
-        s0[...] = x[:, :, 0:128]
-        s1[...] = jnp.concatenate([x[:, :, 128:160], jnp.zeros((48, 8, 96), F32)], 2)
-        for half in range(2):
-            rows4 = [jnp.concatenate([s0[:, half * 4 + h, :], s1[:, half * 4 + h, :]], 1) for h in range(4)]
-            for to in range(NW):
-                got = None
-                for h in range(4):
-                    shift = (half * 128 + h * 32 - (20 * to - 3)) % 256
-                    moved = pltpu.roll(rows4[h], shift, 1)[:, half * 128 : half * 128 + 128]
-                    got = moved if got is None else jnp.where(quarter == h, moved, got)
-                pack[to, t, :, half * 128 : half * 128 + 128] = got.astype(BF)
-
     pl.semaphore_wait(barrier, NW - 1 + NW * (jnp.where(north, 1, 0) + jnp.where(south, 1, 0)))
 
     mine = pl.ds(pl.multiple_of(w * 48, 16), 48)
@@ -216,18 +212,39 @@
     remote(ft.at[:, 31], v_f.at[:, 0], 1, w, south, north)
     remote(ft.at[:, 0], v_f.at[:, 33], -1, w, north, south)
     n_fine = len(copies)
+
+    def begin(first, last):
+        for c, cs, _ in copies[first:last]:
+            if cs is None:
+                c.start()
+            else:
+                pl.when(cs)(c.start)
+
+    begin(0, n_fine)
+
+    odd = lax.rem(a, 2) == 1
+    even = jnp.logical_not(odd)
     for k in range(1, NW):
         to = lax.rem(w + k, NW)
         remote(pack.at[to], v_coarse.at[:, mine, pl.ds(128, 256)], 0, to, None, None)
+    n_main = len(copies)
     for k in range(NW):
         to = lax.rem(w + k, NW)
-        remote(pack.at[to, :, :, pl.ds(128, 128)], v_coarse.at[:, mine, pl.ds(0, 128)], 1, to, south, north)
-        remote(pack.at[to, :, :, pl.ds(0, 128)], v_coarse.at[:, mine, pl.ds(384, 128)], -1, to, north, south)
-    for c, cs, _ in copies:
-        if cs is None:
-            c.start()
-        else:
-            pl.when(cs)(c.start)
+        remote(pack.at[to, :, :, pl.ds(128, 128)], v_coarse.at[:, mine, pl.ds(0, 128)], 1, to,
+               jnp.logical_and(odd, south), jnp.logical_and(even, north))
+        remote(pack.at[to, :, :, pl.ds(0, 128)], v_coarse.at[:, mine, pl.ds(384, 128)], -1, to,
+               jnp.logical_and(even, north), jnp.logical_and(odd, south))
+    n_far = len(copies)
+    remote(v_coarse.at[:, :, pl.ds(256, 128)], v_coarse.at[:, :, pl.ds(0, 128)], 1, w, even, odd)
+    remote(v_coarse.at[:, :, pl.ds(128, 128)], v_coarse.at[:, :, pl.ds(384, 128)], -1, w, odd, even)
+    begin(n_fine, n_far)
+    d_uk = load(uk, v_uk)
+    d_nk = load(nk, v_nk)
+    d_fk = load(fk, v_fk)
+    d_mf = load(mk.at[:, :, :, pl.ds(0, 128), :], v_mf)
+    d_mh = load(mk.at[:, :, :, pl.ds(128, 64), :], v_mh)
+    d_bk = load(bk, v_bk)
+    d_ck = [load(ck.at[t], v_ck.at[t]) for t in range(3)]
 
     def arrived(first, last):
         for c, _, cr in copies[first:last]:
@@ -241,14 +258,36 @@
         v[...].reshape(1, -1) for v in (g_c, b_c, b_u, g_m, b_m, b_b, b_n, g_f, b_f)]
     mbias = mbias + bbias
 
+    xfh[:, 128:256] = jnp.zeros((2560, 128), BF)
+    xmh[:, 128:256] = jnp.zeros((864, 128), BF)
     img1[...] = jnp.zeros_like(img1)
     rb_m[...] = jnp.zeros_like(rb_m)
     rb_1[...] = jnp.zeros_like(rb_1)
     img_m[...] = jnp.zeros_like(img_m)
 
     d_uk.wait()
+    fold_weights(v_uk, w4u)
     d_nk.wait()
+    fold_weights(v_nk, w4n)
     d_fk.wait()
+    pack_fine(v_fk, wfc, wf2)
+
+    def fine_cached(r, beside):
+        buf = rb_f.at[r % 2]
+        for t in range(2):
+            buf[t, 8:88, :] = v_f[t, r].astype(F32)
+            if beside:
+                buf[t, 7:8, :] = lf[t, r : r + 1, :]
+                buf[t, 88:89, :] = rf[t, r : r + 1, :]
+        put_cached(xfc, r * 80, 80, buf, 7)
+
+    rb_f[...] = jnp.zeros_like(rb_f)
+    xfc[0:80, :] = jnp.zeros((80, 1152), BF)
+    xfc[2640:2720, :] = jnp.zeros((80, 1152), BF)
+    for i in range(4):
+        for r in range(8 * i + 2 if i else 1, min(8 * i + 10, 33)):
+            fine_cached(r, False)
+        acc_f[i * 640 : i * 640 + 640, :] = nt_dot(taps(xfc, i * 640, 640, 80), wfc[...]) + fbias
     d_mf.wait()
     d_mh.wait()
     d_bk.wait()
@@ -280,6 +319,21 @@
                 m[t, c, 2:18, :] = g32[t, base + 32 + 16 * c : base + 48 + 16 * c, :]
                 m[t, c, 18:20, :] = g32[t, s + 1 + 2 * c : s + 3 + 2 * c, :]
 
+    for r in (0, 33):
+        fine_cached(r, True)
+    acc_f[0:80, :] += nt_dot(xfc[0:80, :], wfc[:, 0:1152])
+    acc_f[2480:2560, :] += nt_dot(xfc[2640:2720, :], wfc[:, 2304:3456])
+    own_row = lax.broadcasted_iota(jnp.int32, (40, 1), 0)
+    own_row = (own_row >= 1) & (own_row <= 32)
+    for l, col, b in ((lf, 0, 0), (rf, 79, 2)):
+        beside = jnp.zeros((32, 192), F32)
+        for t in range(2):
+            v = jnp.where(own_row, l[t], 0.0)
+            for ra in range(3):
+                beside = beside + nt_dot(v[ra : ra + 32].astype(BF), v_fk[t, ra, b])
+        for h in range(32):
+            acc_f[h * 80 + col : h * 80 + col + 1, :] += beside[h : h + 1]
+
     for r in range(20):
         buf = rb_m.at[r % 2]
         for t in range(2):
@@ -289,32 +343,16 @@
                 buf[t, 48 + c : 49 + c, :] = rm[t, c, r : r + 1, :]
         put_cached(xmc, r * 48, 48, buf, 6)
 
-    def mid_part(i):
-        at = i * 288
+    def mid_part(at, n):
         k = jnp.concatenate(
             [v[t, r, b] for r in range(3) for v in (v_mf, v_mh) for t in range(2) for b in range(3)], 0)
-        acc_m[pl.ds(at, 288), :] = jnp.dot(taps(xmc, at, 288, 48), k, preferred_element_type=F32) + mbias
-
-    for i in range(3):
-        mid_part(i)
-    fold_weights(v_uk, w4u)
-    fold_weights(v_nk, w4n)
-    pack_fine(v_fk, wfc, wf2)
-
-    def fine_cached(r):
-        buf = rb_f.at[r % 2]
-        for t in range(2):
-            buf[t, 8:88, :] = v_f[t, r].astype(F32)
-            buf[t, 7:8, :] = lf[t, r : r + 1, :]
-            buf[t, 88:89, :] = rf[t, r : r + 1, :]
-        put_cached(xfc, r * 80, 80, buf, 7)
-
-    for i in range(4):
-        for r in range(8 * i + 2 if i else 0, 8 * i + 10):
-            fine_cached(r)
-        acc_f[i * 640 : i * 640 + 640, :] = nt_dot(taps(xfc, i * 640, 640, 80), wfc[...]) + fbias
-
-    arrived(n_fine, len(copies))
+        acc_m[at : at + n, :] = jnp.dot(taps(xmc, at, n, 48), k, preferred_element_type=F32) + mbias
+
+    mid_part(0, 864)
+    arrived(n_fine, n_main)
+    begin(n_far, len(copies))
+
+    arrived(n_main, len(copies))
     for t in range(3):
         d_ck[t].wait()
     lane = lax.broadcasted_iota(jnp.int32, (1, 512), 1)
@@ -358,43 +396,37 @@
         ok = jnp.where((row >= 0) & (row < 256), 1.0, 0.0)
         buf = rb_1.at[r % 4]
         buf[0:72, :] = act(image_row(img_m, r + 1, slice(0, 72)), mgain, 192) * (mcol * ok)
-        put_current(xm2, r * 48, 48, buf, 6)
+        put_current(xm2, xmh, r, 18, 48, buf, 6)
 
     def bypass_row(r):
         xmc[r * 48 : r * 48 + 48, 768:960] = image_row(img_m, r + 2, slice(7, 55)).astype(BF)
 
     def mid_block(i):
-        at = i * 288
-        zero = jnp.zeros((64, 384), BF)
+        at = i * 432
         k = jnp.concatenate(
             [p for r in range(3) for p in
-             [v_mf[2, r, b] for b in range(3)] + [v_mh[2, r, b] for b in range(3)] + [zero]], 0)
-        total = (acc_m[pl.ds(at, 288), :]
-                 + jnp.dot(xmc[pl.ds(at, 288), 768:960], v_bk[...], preferred_element_type=F32)
-                 + jnp.dot(taps(xm2, at, 288, 48), k, preferred_element_type=F32))
-        rid = lax.broadcasted_iota(jnp.int32, (6, 48, 1), 0) + (a * 16 - 1 + i * 6)
-        cid = lax.broadcasted_iota(jnp.int32, (6, 48, 1), 1) + (w * 40 - 1)
+             [v_mf[2, r, b] for b in range(3)] + [v_mh[2, r, b] for b in range(2)]]
+            + [v_mh[2, r, 2] for r in range(3)] + [jnp.zeros((64, 384), BF)], 0)
+        x = jnp.concatenate([taps(xm2, at, 432, 48), xmh[at : at + 432, :]], 1)
+        total = (acc_m[at : at + 432, :]
+                 + jnp.dot(xmc[at : at + 432, 768:960], v_bk[...], preferred_element_type=F32)
+                 + jnp.dot(x, k, preferred_element_type=F32))
+        rid = lax.broadcasted_iota(jnp.int32, (9, 48, 1), 0) + (a * 16 - 1 + i * 9)
+        cid = lax.broadcasted_iota(jnp.int32, (9, 48, 1), 1) + (w * 40 - 1)
         inside = (rid >= 0) & (rid < 256) & (cid >= 0) & (cid < 320)
-        img2[i * 6 : i * 6 + 6, 0:48, :] = jnp.where(inside, total.reshape(6, 48, 384), 0.0)
-        for r in range(i * 6, i * 6 + 6):
+        img2[i * 9 : i * 9 + 9, 0:48, :] = jnp.where(inside, total.reshape(9, 48, 384), 0.0)
+        for r in range(i * 9, i * 9 + 9):
             for b in range(2):
                 xmc[r * 48 : r * 48 + 48, b * 384 : b * 384 + 384] = img2[r, b : b + 48, :].astype(BF)
 
-    xmc[864:912, 0:768] = jnp.zeros((48, 768), BF)
-    for i in range(3):
-        for r in range(6 * i + 2 if i else 0, 6 * i + 8):
-            mid_row(r)
-        for r in range(6 * i, 6 * i + 6):
-            bypass_row(r)
-        mid_block(i)
-
-    def fine_block(i):
-        at = i * 288
-        x = jnp.concatenate([xmc[at : at + 288, 0:768], xmc[at + 48 : at + 336, 0:768]], 1)
+    def fine_block(first, n):
+        at, m = first * 48, n * 48
+        x = jnp.concatenate([xmc[at : at + m, 0:768], xmc[at + 48 : at + 48 + m, 0:768]], 1)
         u = nt_dot(x, w4n[...])
-        for j in range(6):
-            put_phases(u[j * 48 : j * 48 + 48, :], nbias, img_f, i * 12 + 2 * j, 7)
-
+        for j in range(n):
+            put_phases(u[j * 48 : j * 48 + 48, :], nbias, img_f, 2 * (first + j), 7)
+
+    dones = []
     fcol = lax.broadcasted_iota(jnp.int32, (96, 1), 0) + (w * 80 - 8)
     fcol = jnp.where((fcol >= 0) & (fcol < 640), 1.0, 0.0)
 
@@ -404,39 +436,52 @@
             ok = jnp.where((row >= 0) & (row < 512), 1.0, 0.0)
             buf = rb_1.at[r % 4]
             buf[0:96, :] = act(image_row(img_f, r, slice(0, 96)), fgain, 192) * (fcol * ok)
-            put_current(xf2, r * 80, 80, buf, 7)
+            put_current(xf2, xfh, r, 32, 80, buf, 7)
 
     def out_block(i):
         at = i * 640
         total = (image_row(img_f, slice(1 + i * 8, 9 + i * 8), slice(8, 88)).reshape(640, 192)
-                 + acc_f[at : at + 640, :] + nt_dot(taps(xf2, at, 640, 80), wf2[...]))
+                 + acc_f[at : at + 640, :] + nt_dot(
+                     jnp.concatenate([taps(xf2, at, 640, 80), xfh[at : at + 640, :]], 1), wf2[...]))
         v_f[0, i * 8 : i * 8 + 8] = total.reshape(8, 80, 192).astype(BF)
-
-    fine_block(0)
-    fine_block(1)
-    fine_rows(0, 12)
-    fine_block(2)
+        rows = pl.ds(i * 8, 8)
+        done = pltpu.make_async_copy(v_f.at[0, rows], out.at[rows], osem.at[i])
+        done.start()
+        dones.append(done)
+
+    for r in range(11):
+        mid_row(r)
+    for r in range(9):
+        bypass_row(r)
+    mid_block(0)
+    for r in range(11, 20):
+        mid_row(r)
+    for r in range(9, 18):
+        bypass_row(r)
+    fine_block(0, 8)
+    mid_block(1)
+    fine_rows(0, 16)
+    fine_block(8, 9)
     out_block(0)
-    fine_rows(12, 24)
+    fine_rows(16, 26)
     out_block(1)
-    fine_rows(24, 34)
+    fine_rows(26, 34)
     out_block(2)
     out_block(3)
-    done = pltpu.make_async_copy(v_f.at[0, pl.ds(0, 32)], out, osem)
-    done.start()
     for c, cs, _ in copies:
         if cs is None:
             c.wait_send()
         else:
             pl.when(cs)(c.wait_send)
-    done.wait()
+    for done in dones:
+        done.wait()
 
 
 def call(*args):
     anywhere = pl.BlockSpec(memory_space=pl.ANY)
     vmem = pl.BlockSpec(memory_space=pltpu.VMEM)
     V = pltpu.VMEM
-    n = 10 + 7 + 16
+    n = 10 + 7 + 16 + 2
     return pl.pallas_call(
         kernel,
         out_shape=jax.ShapeDtypeStruct((32, 80, 192), BF),
@@ -448,14 +493,14 @@
             V((3, 3, 3, 128, 384), BF), V((3, 3, 3, 64, 384), BF),
             V((192, 384), BF), V((3, 3, 192, 384), BF), V((3, 3, 3, 192, 192), BF),
             V((48, 8, 128), F32), V((48, 8, 128), F32), V((2, 192, 192), F32), V((2, 192, 192), BF), V((8, 3, 48, 256), BF),
-            V((192, 3456), BF), V((192, 1920), BF), V((768, 1536), BF), V((768, 1536), BF),
-            V((2720, 1152), BF), V((2720, 640), BF), V((960, 1152), BF), V((960, 640), BF),
+            V((192, 3456), BF), V((192, 1792), BF), V((768, 1536), BF), V((768, 1536), BF),
+            V((2720, 1152), BF), V((2720, 512), BF), V((2560, 256), BF), V((960, 1152), BF), V((960, 512), BF), V((864, 256), BF),
             V((16, 40, 384), F32), V((16, 32, 384), F32), V((12, 40, 384), F32), V((2, 22, 72, 128), F32),
-            V((18, 56, 384), F32), V((2, 36, 104, 128), F32), V((2, 2, 96, 192), F32), V((2, 2, 72, 192), F32),
+            V((18, 56, 384), F32), V((2, 34, 104, 128), F32), V((2, 2, 96, 192), F32), V((2, 2, 72, 192), F32),
             V((4, 96, 192), F32), V((2, 192, 192), F32),
             V((2, 40, 192), F32), V((2, 40, 192), F32), V((2, 2, 24, 192), F32), V((2, 2, 24, 192), F32),
             V((2560, 192), F32), V((864, 384), F32),
-            pltpu.SemaphoreType.DMA((16,)), pltpu.SemaphoreType.DMA,
+            pltpu.SemaphoreType.DMA((16,)), pltpu.SemaphoreType.DMA((4,)),
             pltpu.SemaphoreType.DMA((n,)), pltpu.SemaphoreType.DMA((n,)),
         ],
         compiler_params=pltpu.CompilerParams(

time: 49.2 us -> 44.2 us (0.90)
  the two profiles are of different devices: /device:TPU:99 before, /device:TPU:7 now
where the time goes in v2:
time: 44.2 us; the launch traced here: 44.1 us
  Pallas kernels  41.6 us (94%)
  local copies, waits for them, and re-layouts  2.46 us (6%)
    pallas_call x1, Pallas kernels, call(): pl.pallas_call(kernel, out_shape=jax.ShapeDtypeStruct((32, 80, 192), BF),...  41.6 us
    unnamed x1, local copies, waits for them, and re-layouts  2.46 us

profile of v2, /device:TPU:7, one launch (start us, length us, event | category | flops | bytes accessed | tf_op | source)
XLA Modules:
  0.0 44.1 jit_solution(6239629785584175014)
XLA Ops:
  0.0 41.6 %shard_map.181 = bf16[32,80,192]{2,1,0:T(8,128)(2,1)} custom-call(bf16[48,8,160]{2,1,0:T(8,128)(2,1)} %lat.1, bf16[2,48,8,160]{3,2,1,0:T(8,128)(2,1)} %cc.1, f32[384]{0:T(512)} %g_c.1, f32[384]{0:T(512)} %b_c.1, f32[192]{0:T(256)} %b_u.1, f32[192]{0:T(256)} %g_m.1, f32[384]{0:T(512)} %b_m.1, f32[384]{0:T(512)} %b_b.1, f32[192]{0:T(256)} %b_n.1, f32[192]{0:T(256)} %g_f.1, ...), custom_call_target="tpu_custom_call" | custom-call | tf_op jit(solution)/shard_map/pallas_call | solution.py:485
  41.6 2.5 %copy.21 = bf16[192,32,80]{0,2,1:T(8,128)(2,1)} copy(bf16[192,32,80]{0,2,1:T(8,128)(2,1)} %bitcast.5) | data formatting | bytes 1966080
